TPU v7x, 32 devices: a whole 2x2x4 slice. The times are simulated.
32 devices in a mesh: seq: 8 (over z, x), batch: 4 (over y, core).
Axes of the slice: x: 2, y: 2, z: 4, core: 2. Of those that a mesh axis runs over, the one named last changes fastest.
Arguments:
- tokens: bfloat16 [8, 2048, 1024], P('batch', 'seq'), may hold values from -6 to 6
- cotangent: bfloat16 [8, 2048, 1024], P('batch', 'seq'), may hold values from -6 to 6
- gate_weight: bfloat16 [1024, 1536], replicated, may hold values from -0.1875 to 0.1875
- branch_weight: bfloat16 [1024, 1536], replicated, may hold values from -0.1875 to 0.1875
- out_weight: bfloat16 [1536, 1024], replicated, may hold values from -0.4375 to 0.4375
- conv_taps: float32 [4, 1536], replicated, may hold values from -3 to 3
- conv_offset: float32 [1536], replicated, may hold values from -3 to 3
- rate_weight: bfloat16 [16, 96, 96], replicated, may hold values from -0.625 to 0.625
- inlet_weight: bfloat16 [16, 96, 96], replicated, may hold values from -0.625 to 0.625
- rate_offset: float32 [1536], replicated, may hold values from -4 to 4
- inlet_offset: float32 [1536], replicated, may hold values from -4 to 4
- decay_param: float32 [1536], replicated, may hold values from -14 to -3.8, as said below
- mixer_gain: float32 [1024], replicated, may hold values from 0.5 to 1.5
- feed_gain: float32 [1024], replicated, may hold values from 0.5 to 1.5
- feed_gate: bfloat16 [1024, 3072], replicated, may hold values from -0.1875 to 0.1875
- feed_up: bfloat16 [1024, 3072], replicated, may hold values from -0.1875 to 0.1875
- feed_down: bfloat16 [3072, 1024], replicated, may hold values from -0.15625 to 0.15625
Outputs:
- block_out: bfloat16 [8, 2048, 1024], P('batch', 'seq')
- tokens_grad: float32 [8, 2048, 1024], P('batch', 'seq')
- gate_grad: float32 [1024, 1536], P('seq')
- branch_grad: float32 [1024, 1536], P('seq')
- out_grad: float32 [1536, 1024], P('seq')
- taps_grad: float32 [4, 1536], replicated
- offset_conv: float32 [1536], replicated
- rate_grad: float32 [16, 96, 96], replicated
- inlet_grad: float32 [16, 96, 96], replicated
- offset_rate: float32 [1536], replicated
- offset_inlet: float32 [1536], replicated
- decay_grad: float32 [1536], replicated
- gain_mixer: float32 [1024], replicated
- gain_feed: float32 [1024], replicated
- gate_feed: float32 [1024, 3072], P('seq')
- up_feed: float32 [1024, 3072], P('seq')
- down_feed: float32 [3072, 1024], P('seq')
Inputs may be any that keep to these rules, and one draw needn't show every extreme that they name: `decay_param`: softplus of each entry lies between 0.05 / 2048 and 0.02.
All inputs are finite; a program needn't handle non-finite values.
Results may differ from a plain program's by a relative error of at most 0.012.
Values may be sent and summed in bfloat16 or wider, within the bound.
A program may use at most 256 MiB of HBM per device.

v0:
```python
import jax
import jax.numpy as jnp
from jax import lax
from jax.sharding import PartitionSpec as P


def from_behind(value, axis, steps):
    count = lax.axis_size(axis)
    initial, last = (max(0, -steps), min(count, count - steps))
    return lax.ppermute(value, axis, [(source, source + steps) for source in range(initial, last)])


def carried_in(part, axis, combine, identity, reverse):
    count = lax.axis_size(axis)
    place = lax.axis_index(axis)
    ahead = count - 1 - place if reverse else place
    gathered = jax.tree.map(lambda a: lax.all_gather(a, axis), part)
    state = jax.tree.map(lambda a, e: jnp.zeros_like(a) + jnp.asarray(e, a.dtype), part, identity)

    def one(lap, state):
        source = count - 1 - lap if reverse else lap
        return combine(
            state, jax.tree.map(lambda a: lax.dynamic_index_in_dim(a, source, 0, False), gathered)
        )

    return lax.fori_loop(0, ahead, one, state)


def rms_norm(values, gain):
    scale = lax.rsqrt(jnp.mean(values * values, axis=-1, keepdims=True) + 1e-06)
    return values * scale * gain


def combine(earlier, later):
    return (earlier[0] * later[0], later[0] * earlier[1] + later[1])


def matmul(left, right):
    return jnp.dot(left, right, preferred_element_type=jnp.float32)


def outer_product(left, right):
    return lax.dot_general(
        left, right, (((0,), (0,)), ((), ())), preferred_element_type=jnp.float32
    )


def back_product(grads, weight):
    return lax.dot_general(
        grads, weight, (((1,), (1,)), ((), ())), preferred_element_type=jnp.float32
    )


def convolve(extended, conv_taps, conv_offset):
    local_len = extended.shape[1] - 3
    total = conv_offset + conv_taps[0] * extended[:, 3 : 3 + local_len]
    for tap_index in range(1, 4):
        total = (
            total + conv_taps[tap_index] * extended[:, 3 - tap_index : 3 - tap_index + local_len]
        )
    return total


def gate_values(rate_prod, inlet_prod, mixed_values, rate_offset, inlet_offset, decay_param):
    rate = jax.nn.sigmoid(rate_prod + rate_offset)
    inlet = jax.nn.sigmoid(inlet_prod + inlet_offset)
    log_decay = -8.0 * rate * jax.nn.softplus(decay_param)
    decay = jnp.exp(log_decay)
    drive = jnp.sqrt(-jnp.expm1(2.0 * log_decay)) * inlet * mixed_values
    return (decay, drive)


def gated_gelu(up_gate, up_value):
    return jax.nn.gelu(up_gate) * up_value


def local(
    tokens,
    cotangent,
    gate_weight,
    branch_weight,
    out_weight,
    conv_taps,
    conv_offset,
    rate_weight,
    inlet_weight,
    rate_offset,
    inlet_offset,
    decay_param,
    mixer_gain,
    feed_gain,
    feed_gate,
    feed_up,
    feed_down,
):
    seq_count, local_len, model_width = tokens.shape
    lru_width = gate_weight.shape[1]
    block_count, block_width = (rate_weight.shape[0], rate_weight.shape[1])
    row_count = seq_count * local_len
    source = tokens.reshape(row_count, model_width).astype(jnp.float32)
    normed_full, norm_pull = jax.vjp(rms_norm, source, mixer_gain)
    normed = normed_full.astype(jnp.bfloat16)
    gate_pre = matmul(normed, gate_weight)
    branch = (
        matmul(normed, branch_weight).astype(jnp.bfloat16).reshape(seq_count, local_len, lru_width)
    )
    left_edge = from_behind(branch[:, local_len - 3 :, :], "seq", 1)
    extended = jnp.concatenate([left_edge, branch], axis=1)
    convolved, conv_pull = jax.vjp(convolve, extended.astype(jnp.float32), conv_taps, conv_offset)
    mixed = convolved.astype(jnp.bfloat16)
    mixed_blocks = mixed.reshape(row_count, block_count, block_width)
    rate_prod = jnp.einsum(
        "tbi,bio->tbo", mixed_blocks, rate_weight, preferred_element_type=jnp.float32
    )
    inlet_prod = jnp.einsum(
        "tbi,bio->tbo", mixed_blocks, inlet_weight, preferred_element_type=jnp.float32
    )
    rate_prod = rate_prod.reshape(seq_count, local_len, lru_width)
    inlet_prod = inlet_prod.reshape(seq_count, local_len, lru_width)
    (decay, drive), gate_pull = jax.vjp(
        gate_values,
        rate_prod,
        inlet_prod,
        mixed.astype(jnp.float32),
        rate_offset,
        inlet_offset,
        decay_param,
    )
    cum_decay, local_states = lax.associative_scan(combine, (decay, drive), axis=1)
    unit_rows = jnp.ones((seq_count, lru_width), jnp.float32)
    empty_rows = jnp.zeros((seq_count, lru_width), jnp.float32)
    entry = carried_in(
        (cum_decay[:, -1], local_states[:, -1]), "seq", combine, (unit_rows, empty_rows), False
    )
    states = local_states + cum_decay * entry[1][:, None, :]
    state_rows = states.reshape(row_count, lru_width)
    gate_act, gelu_pull = jax.vjp(jax.nn.gelu, gate_pre)
    joined = (gate_act * state_rows).astype(jnp.bfloat16)
    resid = source + matmul(joined, out_weight)
    normed_two_full, norm_two_pull = jax.vjp(rms_norm, resid, feed_gain)
    normed_two = normed_two_full.astype(jnp.bfloat16)
    up_gate = matmul(normed_two, feed_gate)
    up_value = matmul(normed_two, feed_up)
    hidden_full, glu_pull = jax.vjp(gated_gelu, up_gate, up_value)
    hidden = hidden_full.astype(jnp.bfloat16)
    block_out = (
        (resid + matmul(hidden, feed_down))
        .astype(jnp.bfloat16)
        .reshape(seq_count, local_len, model_width)
    )
    grad_rows = cotangent.reshape(row_count, model_width)
    down_sum = outer_product(hidden, grad_rows)
    grad_hidden = back_product(grad_rows, feed_down)
    grad_upgate, grad_upvalue = glu_pull(grad_hidden)
    upgate_low = grad_upgate.astype(jnp.bfloat16)
    upvalue_low = grad_upvalue.astype(jnp.bfloat16)
    gatefeed_sum = outer_product(normed_two, upgate_low)
    upfeed_sum = outer_product(normed_two, upvalue_low)
    grad_normed_two = back_product(upgate_low, feed_gate) + back_product(upvalue_low, feed_up)
    resid_part, feed_gain_sum = norm_two_pull(grad_normed_two)
    grad_resid = grad_rows.astype(jnp.float32) + resid_part
    resid_low = grad_resid.astype(jnp.bfloat16)
    out_sum = outer_product(joined, resid_low)
    grad_joined = back_product(resid_low, out_weight)
    again = carried_in(
        (cum_decay[:, -1], local_states[:, -1]), "seq", combine, (unit_rows, empty_rows), False
    )
    entry_back = again[1]
    states_back = local_states + cum_decay * entry_back[:, None, :]
    grad_gate_pre = gelu_pull(grad_joined * states_back.reshape(row_count, lru_width))[0].astype(
        jnp.bfloat16
    )
    grad_states = (grad_joined * gate_act).reshape(seq_count, local_len, lru_width)
    shifted = jnp.concatenate(
        [decay[:, 1:], jnp.ones((seq_count, 1, lru_width), jnp.float32)], axis=1
    )
    back_cum, local_grads = lax.associative_scan(
        combine, (shifted, grad_states), reverse=True, axis=1
    )
    first_decay = decay[:, 0]
    carried = carried_in(
        (first_decay * back_cum[:, 0], first_decay * local_grads[:, 0]),
        "seq",
        combine,
        (unit_rows, empty_rows),
        True,
    )
    state_grads = local_grads + back_cum * carried[1][:, None, :]
    previous = jnp.concatenate([entry_back[:, None, :], states_back[:, :-1]], axis=1)
    (
        grad_rate_prod,
        grad_inlet_prod,
        grad_mixed_direct,
        rate_offset_sum,
        inlet_offset_sum,
        decay_sum,
    ) = gate_pull((state_grads * previous, state_grads))
    rate_low = grad_rate_prod.astype(jnp.bfloat16).reshape(row_count, block_count, block_width)
    inlet_low = grad_inlet_prod.astype(jnp.bfloat16).reshape(row_count, block_count, block_width)
    rate_sum = jnp.einsum(
        "tbi,tbo->bio", mixed_blocks, rate_low, preferred_element_type=jnp.float32
    )
    inlet_sum = jnp.einsum(
        "tbi,tbo->bio", mixed_blocks, inlet_low, preferred_element_type=jnp.float32
    )
    mixed_back = jnp.einsum(
        "tbo,bio->tbi", rate_low, rate_weight, preferred_element_type=jnp.float32
    )
    mixed_back = mixed_back + jnp.einsum(
        "tbo,bio->tbi", inlet_low, inlet_weight, preferred_element_type=jnp.float32
    )
    grad_mixed = grad_mixed_direct + mixed_back.reshape(seq_count, local_len, lru_width)
    grad_extended, taps_sum, conv_offset_sum = conv_pull(grad_mixed)
    back_edge = from_behind(grad_extended[:, :3], "seq", -1)
    grad_branch = grad_extended[:, 3:].at[:, local_len - 3 :].add(back_edge)
    branch_low = grad_branch.reshape(row_count, lru_width).astype(jnp.bfloat16)
    branch_sum = outer_product(normed, branch_low)
    gate_sum = outer_product(normed, grad_gate_pre)
    grad_normed = back_product(grad_gate_pre, gate_weight) + back_product(branch_low, branch_weight)
    source_part, mixer_gain_sum = norm_pull(grad_normed)
    tokens_grad = (grad_resid + source_part).reshape(seq_count, local_len, model_width)
    small_sums = lax.psum(
        (
            taps_sum,
            conv_offset_sum,
            rate_sum,
            inlet_sum,
            rate_offset_sum,
            inlet_offset_sum,
            decay_sum,
            mixer_gain_sum,
            feed_gain_sum,
        ),
        ("seq", "batch"),
    )
    row_parts = (
        lax.psum_scatter(gate_sum, "seq", scatter_dimension=0, tiled=True),
        lax.psum_scatter(branch_sum, "seq", scatter_dimension=0, tiled=True),
        lax.psum_scatter(out_sum, "seq", scatter_dimension=0, tiled=True),
        lax.psum_scatter(gatefeed_sum, "seq", scatter_dimension=0, tiled=True),
        lax.psum_scatter(upfeed_sum, "seq", scatter_dimension=0, tiled=True),
        lax.psum_scatter(down_sum, "seq", scatter_dimension=0, tiled=True),
    )
    summed = lax.psum(
        (row_parts[0], row_parts[1], row_parts[2], row_parts[3], row_parts[4], row_parts[5]),
        "batch",
    )
    return (
        block_out,
        tokens_grad,
        summed[0],
        summed[1],
        summed[2],
        small_sums[0],
        small_sums[1],
        small_sums[2],
        small_sums[3],
        small_sums[4],
        small_sums[5],
        small_sums[6],
        small_sums[7],
        small_sums[8],
        summed[3],
        summed[4],
        summed[5],
    )


def solution(mesh):
    in_specs = (
        P("batch", "seq", None),
        P("batch", "seq", None),
        P(),
        P(),
        P(),
        P(),
        P(),
        P(),
        P(),
        P(),
        P(),
        P(),
        P(),
        P(),
        P(),
        P(),
        P(),
    )
    out_specs = (
        P("batch", "seq", None),
        P("batch", "seq", None),
        P("seq", None),
        P("seq", None),
        P("seq", None),
        P(),
        P(),
        P(),
        P(),
        P(),
        P(),
        P(),
        P(),
        P(),
        P("seq", None),
        P("seq", None),
        P("seq", None),
    )
    return jax.shard_map(local, mesh=mesh, in_specs=in_specs, out_specs=out_specs, check_vma=False)
```

profile of v0, /device:TPU:0, one launch (start us, length us, event | category | flops | bytes accessed | tf_op | source)
XLA Modules:
  0.0 1758.0 jit_solution(3595095496055897608)
XLA Ops:
  66.9 10.9 convert_multiply_fusion.1
  79.4 7.7 slice.626
  87.2 7.6 slice.572
  94.8 7.6 slice.571
  111.4 7.6 slice.570
  192.1 7.8 slice.569
  290.7 32.6 %all-gather = f32[16,1,1536]{2,1,0:T(1,128)S(1)} all-gather(f32[2,1,1536]{2,1,0:T(1,128)S(1)} %slice_add_fusion.3), channel_id=2, replica_groups=mesh['seq'=8,'batch'=4] {'seq'}, dimensions={0}, use_global_device_ids=true | all-gather | bytes 110592 | tf_op jit(solution)/shard_map/all_gather | solution.py:17
  339.9 30.5 %all-gather.1 = f32[16,1,1536]{2,1,0:T(1,128)S(1)} all-gather(f32[2,1,1536]{2,1,0:T(1,128)S(1)} %slice_add_fusion.2), channel_id=3, replica_groups=mesh['seq'=8,'batch'=4] {'seq'}, dimensions={0}, use_global_device_ids=true | all-gather | bytes 110592 | tf_op jit(solution)/shard_map/all_gather | solution.py:17
  396.3 15.0 multiply_convert_fusion
  452.9 7.7 slice.708
  469.3 12.9 slice.656
  482.2 8.0 slice.649
  490.2 12.9 slice.651
  503.0 7.9 slice.653
  570.8 7.9 slice.647
  578.8 8.1 slice.709
  639.4 24.8 %rev.8 = f32[2,256,1536]{2,1,0:T(8,128)} reverse(f32[2,256,1536]{2,1,0:T(8,128)} %add.616), dimensions={1} | reverse | bytes 6291456 | tf_op jit(solution)/shard_map/rev | solution.py:177
  677.9 24.9 %rev.9 = f32[2,256,1536]{2,1,0:T(8,128)} reverse(f32[2,256,1536]{2,1,0:T(8,128)} %add.624), dimensions={1} | reverse | bytes 6291456 | tf_op jit(solution)/shard_map/rev | solution.py:177
  703.9 31.9 %all-gather.3 = f32[16,1,1536]{2,1,0:T(1,128)S(1)} all-gather(f32[2,1,1536]{2,1,0:T(1,128)S(1)} %get-tuple-element.237), channel_id=5, replica_groups=mesh['seq'=8,'batch'=4] {'seq'}, dimensions={0}, use_global_device_ids=true | all-gather | bytes 110592 | tf_op jit(solution)/shard_map/all_gather | solution.py:17
  736.2 30.5 %all-gather.2 = f32[16,1,1536]{2,1,0:T(1,128)S(1)} all-gather(f32[2,1,1536]{2,1,0:T(1,128)S(1)} %get-tuple-element.238), channel_id=4, replica_groups=mesh['seq'=8,'batch'=4] {'seq'}, dimensions={0}, use_global_device_ids=true | all-gather | bytes 110592 | tf_op jit(solution)/shard_map/all_gather | solution.py:17
  773.0 12.2 fusion.66
  827.8 10.9 multiply_reduce_fusion.4
  855.2 8.3 fusion.88
  863.5 8.4 fusion.87
  873.2 8.5 fusion.89
  887.0 85.8 %reduce-scatter.9.cloned.1.call-done = f32[128,1536]{1,0:T(8,128)} async-done(((f32[1024,1536]{1,0:T(8,128)}), f32[128,1536]{1,0:T(8,128)}) %reduce-scatter.9.cloned.1.call-update) | async-done | bytes 786448 | tf_op jit(solution)/shard_map/reduce_scatter | solution.py:238
  972.8 212.7 %reduce-scatter.15.cloned.1.call-done = f32[128,3072]{1,0:T(8,128)} async-done(((f32[1024,3072]{1,0:T(8,128)}), f32[128,3072]{1,0:T(8,128)}) %reduce-scatter.15.cloned.1.call-update) | async-done | bytes 1572880 | tf_op jit(solution)/shard_map/reduce_scatter | solution.py:241
  1185.5 209.9 %reduce-scatter.13.cloned.1.call-done = f32[128,3072]{1,0:T(8,128)} async-done(((f32[1024,3072]{1,0:T(8,128)}), f32[128,3072]{1,0:T(8,128)}) %reduce-scatter.13.cloned.1.call-update) | async-done | bytes 1572880 | tf_op jit(solution)/shard_map/reduce_scatter | solution.py:240
  1395.4 209.9 %reduce-scatter.17.cloned.1.call-done = f32[384,1024]{1,0:T(8,128)} async-done(((f32[3072,1024]{1,0:T(8,128)}), f32[384,1024]{1,0:T(8,128)}) %reduce-scatter.17.cloned.1.call-update) | async-done | bytes 1572880 | tf_op jit(solution)/shard_map/reduce_scatter | solution.py:242
  1610.5 7.6 add_convert_fusion.1
  1621.6 42.9 %all-reduce.74 = (f32[4,1536]{1,0:T(4,128)}, f32[1536]{0:T(1024)}, f32[1536]{0:T(1024)}, f32[1536]{0:T(1024)}, f32[1536]{0:T(1024)}, /*index=5*/f32[1024]{0:T(1024)}, f32[1024]{0:T(1024)}) all-reduce(f32[4,1536]{1,0:T(4,128)S(1)} %pad_add_fusion.6, ...), channel_id=1, replica_groups=mesh['seq'=8,'batch'=4] {'seq','batch'}, use_global_device_ids=true, to_apply=%region_18.19 | all-reduce | flops 14336 | bytes 114688 | tf_op jit(solution)/shard_map/psum | solution.py:222
  1668.0 71.1 %all-reduce.82.cloned.1.call-done = (f32[128,1536]{1,0:T(8,128)}, f32[128,1536]{1,0:T(8,128)}, f32[192,1024]{1,0:T(8,128)}, f32[128,3072]{1,0:T(8,128)}, f32[128,3072]{1,0:T(8,128)}, /*index=5*/f32[384,1024]{1,0:T(8,128)}) async-done(((f32[128,1536]{1,0:T(8,128)}, f32[128,1536]{1,0:T(8,128)}, f32[192,1024]{1,0:T(8,128)}, f32[128,3072]{1,0:T(8,128)}, f32[128,3072]{1,0:T(8,128)}, ...) | async-done | bytes 7077904 | tf_op jit(solution)/shard_map/psum | solution.py:244
  (665 shorter events, 551.9 us)
Async XLA Ops:
  8.0 373.1 %copy-start = (bf16[1536,1024]{1,0:T(8,128)(2,1)S(1)}, bf16[1536,1024]{1,0:T(8,128)(2,1)}, u32[]{:S(2)}) copy-start(bf16[1536,1024]{1,0:T(8,128)(2,1)} %param.27) | copy-start | bytes 9437188
  8.0 878.9 %reduce-scatter.7.cloned.1.call-start = ((), (), s32[]{:S(2)}) async-start(), calls=%async_computation.6 | async-start | bytes 7077888 | tf_op jit(solution)/shard_map/reduce_scatter | solution.py:237
  16.1 6.4 collective-permute-start
  21.7 45.2 %copy-start.80 = (f32[1536]{0:T(1024)}, f32[1536]{0:T(1024)S(1)}, u32[]{:S(2)}) copy-start(f32[1536]{0:T(1024)S(1)} %get-tuple-element.182) | copy-start | bytes 18436
  21.7 45.2 %copy-start.82 = (f32[1536]{0:T(1024)}, f32[1536]{0:T(1024)S(1)}, u32[]{:S(2)}) copy-start(f32[1536]{0:T(1024)S(1)} %get-tuple-element.183) | copy-start | bytes 18436
  377.0 47.0 %copy-start.25 = (f32[2,256,1536]{2,1,0:T(8,128)}, f32[2,256,1536]{2,1,0:T(8,128)S(1)}, u32[]{:S(2)}) copy-start(f32[2,256,1536]{2,1,0:T(8,128)S(1)} %multiply_add_fusion.2) | copy-start | bytes 9437188
  383.1 40.3 %copy-start.30 = (f32[512,1024]{1,0:T(8,128)}, f32[512,1024]{1,0:T(8,128)S(1)}, u32[]{:S(2)}) copy-start(f32[512,1024]{1,0:T(8,128)S(1)} %get-tuple-element.314) | copy-start | bytes 6291460
  437.1 449.9 %reduce-scatter.11.cloned.1.call-start = ((), (), s32[]{:S(2)}) async-start(), calls=%async_computation.8 | async-start | bytes 7077888 | tf_op jit(solution)/shard_map/reduce_scatter | solution.py:239
  469.3 12.9 copy-start.39
  482.2 20.8 %copy-start.40 = (f32[2,128,1536]{2,1,0:T(8,128)S(1)}, f32[2,128,1536]{2,1,0:T(8,128)}, u32[]{:S(2)}) copy-start(f32[2,128,1536]{2,1,0:T(8,128)} %slice.652) | copy-start | bytes 4718596
  534.6 36.2 %copy-start.37 = (f32[2,127,1536]{2,1,0:T(8,128)S(1)}, f32[2,127,1536]{2,1,0:T(8,128)}, u32[]{:S(2)}) copy-start(f32[2,127,1536]{2,1,0:T(8,128)} %slice.646) | copy-start | bytes 4681732
  537.7 41.0 %copy-start.38 = (f32[2,127,1536]{2,1,0:T(8,128)S(1)}, f32[2,127,1536]{2,1,0:T(8,128)}, u32[]{:S(2)}) copy-start(f32[2,127,1536]{2,1,0:T(8,128)} %slice.708) | copy-start | bytes 4681732
  613.4 359.4 %reduce-scatter.9.cloned.1.call-start = ((), (), s32[]{:S(2)}) async-start(), calls=%async_computation.7 | async-start | bytes 7077888 | tf_op jit(solution)/shard_map/reduce_scatter | solution.py:238
  677.8 95.0 %copy-start.4 = (f32[2,256,1536]{2,1,0:T(8,128)S(1)}, f32[2,256,1536]{2,1,0:T(8,128)}, u32[]{:S(2)}) copy-start(f32[2,256,1536]{2,1,0:T(8,128)} %copy.60) | copy-start | bytes 9437188
  677.8 95.1 %copy-start.81 = (f32[1536]{0:T(1024)S(1)}, f32[1536]{0:T(1024)}, u32[]{:S(2)}) copy-start(f32[1536]{0:T(1024)} %copy-done.80) | copy-start | bytes 18436
  677.8 95.1 %copy-start.83 = (f32[1536]{0:T(1024)S(1)}, f32[1536]{0:T(1024)}, u32[]{:S(2)}) copy-start(f32[1536]{0:T(1024)} %copy-done.82) | copy-start | bytes 18436
  677.8 95.1 %copy-start.86 = (f32[1536]{0:T(1024)S(1)}, f32[1536]{0:T(1024)}, u32[]{:S(2)}) copy-start(f32[1536]{0:T(1024)} %copy-done.84) | copy-start | bytes 18436
  677.8 95.1 %copy-start.90 = (f32[1536]{0:T(1024)S(1)}, f32[1536]{0:T(1024)}, u32[]{:S(2)}) copy-start(f32[1536]{0:T(1024)} %copy-done.88) | copy-start | bytes 18436
  677.8 95.1 %copy-start.93 = (f32[1536]{0:T(1024)S(1)}, f32[1536]{0:T(1024)}, u32[]{:S(2)}) copy-start(f32[1536]{0:T(1024)} %get-tuple-element.308) | copy-start | bytes 18436
  677.9 95.1 %copy-start.96 = (f32[1536]{0:T(1024)S(1)}, f32[1536]{0:T(1024)}, u32[]{:S(2)}) copy-start(f32[1536]{0:T(1024)} %param.32) | copy-start | bytes 18436
  677.9 95.1 %copy-start.102 = (f32[1536]{0:T(1024)S(1)}, f32[1536]{0:T(1024)}, u32[]{:S(2)}) copy-start(f32[1536]{0:T(1024)} %param.29) | copy-start | bytes 18436
  677.9 95.1 %copy-start.104 = (f32[1536]{0:T(1024)S(1)}, f32[1536]{0:T(1024)}, u32[]{:S(2)}) copy-start(f32[1536]{0:T(1024)} %param.33) | copy-start | bytes 18436
  773.0 12.2 copy-start.3
  840.2 6.0 collective-permute-start.1
  854.0 331.6 %reduce-scatter.15.cloned.1.call-start = ((), (), s32[]{:S(2)}) async-start(), calls=%async_computation.10 | async-start | bytes 14155776 | tf_op jit(solution)/shard_map/reduce_scatter | solution.py:241
  863.5 531.9 %reduce-scatter.13.cloned.1.call-start = ((), (), s32[]{:S(2)}) async-start(), calls=%async_computation.9 | async-start | bytes 14155776 | tf_op jit(solution)/shard_map/reduce_scatter | solution.py:240
  871.9 733.4 %reduce-scatter.17.cloned.1.call-start = ((), (), s32[]{:S(2)}) async-start(), calls=%async_computation.11 | async-start | bytes 14155776 | tf_op jit(solution)/shard_map/reduce_scatter | solution.py:242
  881.7 786.3 %all-reduce.80.cloned.1.call-start = ((), (), s32[]{:S(2)}) async-start(), calls=%async_computation.12 | async-start | bytes 3145728 | tf_op jit(solution)/shard_map/psum | solution.py:222
  886.6 852.4 %all-reduce.82.cloned.1.call-start = ((), (), s32[]{:S(2)}) async-start(), calls=%async_computation.13 | async-start | bytes 14155776 | tf_op jit(solution)/shard_map/psum | solution.py:244
  1618.2 46.3 %copy-start.137 = (f32[1,2,2,128]{3,1,2,0:T(2,128)S(1)}, f32[1,2,2,128]{3,1,2,0:T(2,128)}, u32[]{:S(2)}) copy-start(f32[1,2,2,128]{3,1,2,0:T(2,128)} %copy-done.136) | copy-start | bytes 6148
  1618.2 46.3 %copy-start.12 = (f32[512,1024]{1,0:T(8,128)S(1)}, f32[512,1024]{1,0:T(8,128)}, u32[]{:S(2)}) copy-start(f32[512,1024]{1,0:T(8,128)} %copy-done.10) | copy-start | bytes 6291460
  1667.9 76.3 %copy-start.73 = (f32[16,96,96]{2,1,0:T(8,128)S(1)}, f32[16,96,96]{2,1,0:T(8,128)}, u32[]{:S(2)}) copy-start(f32[16,96,96]{2,1,0:T(8,128)} %get-tuple-element.450) | copy-start | bytes 1769476
  (131 other events, 639.7 us)
Sparse Core Ops, SparseCore 0:
  437.2 118.2 reduce-scatter.6
  613.5 119.0 reduce-scatter.10
  854.1 118.6 reduce-scatter.8
  976.2 209.2 reduce-scatter.14
  1189.0 206.4 reduce-scatter.12
  1398.9 206.4 reduce-scatter.16
Sparse Core Ops, SparseCore 1:
  888.7 258.5 all-reduce.79
  1605.4 133.5 all-reduce.81
where the time goes:
time: 1770 us; the launch traced here: 1760 us
  waiting for transfers between devices  792 us (45%)
  local copies, waits for them, and re-layouts  489 us (28%)
  blocking collectives  169 us (10%)
  other arithmetic  160 us (9%)
  matrix products  123 us (7%)
  between operations  18.3 us (1%)
    reduce_scatter x1, waiting for transfers between devices, local(): lax.psum_scatter(upfeed_sum, 'seq', scatter_dimension=0, tiled=True)  213 us
    reduce_scatter x1, waiting for transfers between devices, local(): lax.psum_scatter(gatefeed_sum, 'seq', scatter_dimension=0, tiled=True)  210 us
    reduce_scatter x1, waiting for transfers between devices, local(): lax.psum_scatter(down_sum, 'seq', scatter_dimension=0, tiled=True)  210 us
    slice x57, local copies, waits for them, and re-layouts, local(): lax.associative_scan(combine, (shifted, grad_states), reverse=True, axis=1)  138 us
    all_gather x4, blocking collectives, carried_in(): gathered = jax.tree.map(lambda a: lax.all_gather(a, axis), part)  126 us
    slice x52, local copies, waits for them, and re-layouts, local(): lax.associative_scan(combine, (decay, drive), axis=1)  105 us
    reduce_scatter x1, waiting for transfers between devices, local(): lax.psum_scatter(branch_sum, 'seq', scatter_dimension=0, tiled=True)  85.8 us
    psum x1, waiting for transfers between devices, local(): lax.psum((row_parts[0], row_parts[1], row_parts[2], row_parts[3], row_par...  71.1 us
  transfers between devices with their start and end apart: 10, of which 7 were waited for; matrix products, arithmetic and copies ran while one was open for 22% of the time, Pallas kernels for 0%

commit v1 on v0

--- a/solution.py
+++ b/solution.py
@@ -220,18 +220,21 @@
     source_part, mixer_gain_sum = norm_pull(grad_normed)
     tokens_grad = (grad_resid + source_part).reshape(seq_count, local_len, model_width)
     small_sums = lax.psum(
-        (
-            taps_sum,
-            conv_offset_sum,
-            rate_sum,
-            inlet_sum,
-            rate_offset_sum,
-            inlet_offset_sum,
-            decay_sum,
-            mixer_gain_sum,
-            feed_gain_sum,
+        lax.psum(
+            (
+                taps_sum,
+                conv_offset_sum,
+                rate_sum,
+                inlet_sum,
+                rate_offset_sum,
+                inlet_offset_sum,
+                decay_sum,
+                mixer_gain_sum,
+                feed_gain_sum,
+            ),
+            "batch",
         ),
-        ("seq", "batch"),
+        "seq",
     )
     row_parts = (
         lax.psum_scatter(gate_sum, "seq", scatter_dimension=0, tiled=True),

time: 1770 us -> 1890 us (1.068)
  waiting for transfers between devices: 792 us -> 897 us
    psum x1, waiting for transfers between devices: 71.1 us -> 149 us  [local(): lax.psum((row_parts[0], row_parts[1], row_parts[2], row_parts[3], row_par...]
    psum x0 -> x1, blocking collectives: none -> 39.3 us  [local(): lax.psum(lax.psum((taps_sum, conv_offset_sum, rate_sum, inlet_sum, rate_o...]
    psum x1, waiting for transfers between devices: 0.01 us -> 33 us  [local(): lax.psum(lax.psum((taps_sum, conv_offset_sum, rate_sum, inlet_sum, rate_o...]
    psum x1, blocking collectives: 42.9 us -> 11.3 us  [local(): lax.psum((taps_sum, conv_offset_sum, rate_sum, inlet_sum, rate_offset_sum...]
  transfers between devices with their start and end apart: 10 -> 10, of which waited for: 7 -> 8; matrix products, arithmetic and copies ran while one was open for 22% -> 21% of each run, Pallas kernels for 0% -> 0%
where the time goes in v1:
time: 1890 us; the launch traced here: 1870 us
  waiting for transfers between devices  897 us (47%)
  local copies, waits for them, and re-layouts  489 us (26%)
  blocking collectives  176 us (9%)
  other arithmetic  160 us (8%)
  matrix products  127 us (7%)
    reduce_scatter x1, waiting for transfers between devices, local(): lax.psum_scatter(upfeed_sum, 'seq', scatter_dimension=0, tiled=True)  210 us
    reduce_scatter x1, waiting for transfers between devices, local(): lax.psum_scatter(down_sum, 'seq', scatter_dimension=0, tiled=True)  210 us
    reduce_scatter x1, waiting for transfers between devices, local(): lax.psum_scatter(gatefeed_sum, 'seq', scatter_dimension=0, tiled=True)  210 us
    psum x1, waiting for transfers between devices, local(): lax.psum((row_parts[0], row_parts[1], row_parts[2], row_parts[3], row_par...  149 us
    slice x57, local copies, waits for them, and re-layouts, local(): lax.associative_scan(combine, (shifted, grad_states), reverse=True, axis=1)  138 us
    all_gather x4, blocking collectives, carried_in(): gathered = jax.tree.map(lambda a: lax.all_gather(a, axis), part)  126 us
    slice x52, local copies, waits for them, and re-layouts, local(): lax.associative_scan(combine, (decay, drive), axis=1)  105 us
    reduce_scatter x1, waiting for transfers between devices, local(): lax.psum_scatter(branch_sum, 'seq', scatter_dimension=0, tiled=True)  83.4 us
  transfers between devices with their start and end apart: 10, of which 8 were waited for; matrix products, arithmetic and copies ran while one was open for 21% of the time, Pallas kernels for 0%

profile of v1, /device:TPU:0, one launch (start us, length us, event | category | flops | bytes accessed | tf_op | source)
XLA Modules:
  0.0 1873.4 jit_solution(2925024631705011009)
XLA Ops:
  66.1 10.8 convert_multiply_fusion.1
  78.6 7.7 slice.626
  93.9 7.6 slice.571
  191.2 7.8 slice.569
  289.7 32.6 %all-gather = f32[16,1,1536]{2,1,0:T(1,128)S(1)} all-gather(f32[2,1,1536]{2,1,0:T(1,128)S(1)} %slice_add_fusion.3), channel_id=2, replica_groups=mesh['seq'=8,'batch'=4] {'seq'}, dimensions={0}, use_global_device_ids=true | all-gather | bytes 110592 | tf_op jit(solution)/shard_map/all_gather | solution.py:17
  338.9 30.6 %all-gather.1 = f32[16,1,1536]{2,1,0:T(1,128)S(1)} all-gather(f32[2,1,1536]{2,1,0:T(1,128)S(1)} %slice_add_fusion.2), channel_id=3, replica_groups=mesh['seq'=8,'batch'=4] {'seq'}, dimensions={0}, use_global_device_ids=true | all-gather | bytes 110592 | tf_op jit(solution)/shard_map/all_gather | solution.py:17
  395.3 14.9 multiply_convert_fusion
  451.8 7.8 slice.708
  468.1 12.9 slice.656
  481.1 8.0 slice.649
  489.1 12.9 slice.651
  502.0 7.9 slice.653
  569.7 7.9 slice.647
  577.7 8.0 slice.709
  638.2 24.8 %rev.8 = f32[2,256,1536]{2,1,0:T(8,128)} reverse(f32[2,256,1536]{2,1,0:T(8,128)} %add.634), dimensions={1} | reverse | bytes 6291456 | tf_op jit(solution)/shard_map/rev | solution.py:177
  676.6 24.9 %rev.9 = f32[2,256,1536]{2,1,0:T(8,128)} reverse(f32[2,256,1536]{2,1,0:T(8,128)} %add.642), dimensions={1} | reverse | bytes 6291456 | tf_op jit(solution)/shard_map/rev | solution.py:177
  702.7 31.9 %all-gather.3 = f32[16,1,1536]{2,1,0:T(1,128)S(1)} all-gather(f32[2,1,1536]{2,1,0:T(1,128)S(1)} %get-tuple-element.246), channel_id=5, replica_groups=mesh['seq'=8,'batch'=4] {'seq'}, dimensions={0}, use_global_device_ids=true | all-gather | bytes 110592 | tf_op jit(solution)/shard_map/all_gather | solution.py:17
  734.9 30.5 %all-gather.2 = f32[16,1,1536]{2,1,0:T(1,128)S(1)} all-gather(f32[2,1,1536]{2,1,0:T(1,128)S(1)} %get-tuple-element.247), channel_id=4, replica_groups=mesh['seq'=8,'batch'=4] {'seq'}, dimensions={0}, use_global_device_ids=true | all-gather | bytes 110592 | tf_op jit(solution)/shard_map/all_gather | solution.py:17
  771.7 12.2 fusion.66
  826.5 10.8 multiply_reduce_fusion.4
  853.6 8.3 fusion.88
  862.0 8.4 fusion.87
  871.6 8.5 fusion.89
  885.1 83.4 %reduce-scatter.9.cloned.1.call-done = f32[128,1536]{1,0:T(8,128)} async-done(((f32[1024,1536]{1,0:T(8,128)}), f32[128,1536]{1,0:T(8,128)}) %reduce-scatter.9.cloned.1.call-update) | async-done | bytes 786448 | tf_op jit(solution)/shard_map/reduce_scatter | solution.py:241
  968.5 210.0 %reduce-scatter.15.cloned.1.call-done = f32[128,3072]{1,0:T(8,128)} async-done(((f32[1024,3072]{1,0:T(8,128)}), f32[128,3072]{1,0:T(8,128)}) %reduce-scatter.15.cloned.1.call-update) | async-done | bytes 1572880 | tf_op jit(solution)/shard_map/reduce_scatter | solution.py:244
  1178.5 209.8 %reduce-scatter.13.cloned.1.call-done = f32[128,3072]{1,0:T(8,128)} async-done(((f32[1024,3072]{1,0:T(8,128)}), f32[128,3072]{1,0:T(8,128)}) %reduce-scatter.13.cloned.1.call-update) | async-done | bytes 1572880 | tf_op jit(solution)/shard_map/reduce_scatter | solution.py:243
  1388.3 210.0 %reduce-scatter.17.cloned.1.call-done = f32[384,1024]{1,0:T(8,128)} async-done(((f32[3072,1024]{1,0:T(8,128)}), f32[384,1024]{1,0:T(8,128)}) %reduce-scatter.17.cloned.1.call-update) | async-done | bytes 1572880 | tf_op jit(solution)/shard_map/reduce_scatter | solution.py:245
  1604.8 7.7 add_convert_fusion.1
  1612.5 148.8 %all-reduce.83.cloned.1.call-done = (f32[128,1536]{1,0:T(8,128)}, f32[128,1536]{1,0:T(8,128)}, f32[192,1024]{1,0:T(8,128)}, f32[16,96,96]{2,1,0:T(8,128)}, f32[1...) async-done(((f32[128,1536]{1,0:T(8,128)}, f32[128,1536]{1,0:T(8,128)}, f32[192,1024]{1,0:T(8,128)}, f32[16,96,96]{2,1,0:T(8,128)}, ...) | async-done | bytes 8257552 | tf_op jit(solution)/shard_map/psum | solution.py:247
  1768.0 11.3 all-reduce.76
  1779.3 39.3 %all-reduce.74 = (f32[4,1536]{1,0:T(4,128)}, f32[1536]{0:T(1024)}, f32[1536]{0:T(1024)}, f32[1536]{0:T(1024)}, f32[1536]{0:T(1024)}, /*index=5*/f32[1024]{0:T(1024)}, f32[1024]{0:T(1024)}) all-reduce(f32[4,1536]{1,0:T(4,128)S(1)} %get-tuple-element.215, ...), channel_id=1, replica_groups=mesh['seq'=8,'batch'=4] {'seq'}, use_global_device_ids=true, to_apply=%region_19.20 | all-reduce | flops 14336 | bytes 114688 | tf_op jit(solution)/shard_map/psum | solution.py:222
  1822.1 33.0 %all-reduce.81.cloned.1.call-done = (f32[16,96,96]{2,1,0:T(8,128)}, f32[16,96,96]{2,1,0:T(8,128)}) async-done(((f32[16,96,96]{2,1,0:T(8,128)}, f32[16,96,96]{2,1,0:T(8,128)}), (f32[16,96,96]{2,1,0:T(8,128)}, f32[16,96,96]{2,1,0:T(8,128)})) %all-reduce.81.cloned.1.call-update) | async-done | bytes 1179664 | tf_op jit(solution)/shard_map/psum | solution.py:222
  (662 shorter events, 570.8 us)
Async XLA Ops:
  7.2 373.0 %copy-start = (bf16[1536,1024]{1,0:T(8,128)(2,1)S(1)}, bf16[1536,1024]{1,0:T(8,128)(2,1)}, u32[]{:S(2)}) copy-start(bf16[1536,1024]{1,0:T(8,128)(2,1)} %param.27) | copy-start | bytes 9437188
  7.2 877.8 %reduce-scatter.7.cloned.1.call-start = ((), (), s32[]{:S(2)}) async-start(), calls=%async_computation.6 | async-start | bytes 7077888 | tf_op jit(solution)/shard_map/reduce_scatter | solution.py:240
  15.2 6.4 collective-permute-start
  20.8 45.2 %copy-start.79 = (f32[1536]{0:T(1024)}, f32[1536]{0:T(1024)S(1)}, u32[]{:S(2)}) copy-start(f32[1536]{0:T(1024)S(1)} %get-tuple-element.182) | copy-start | bytes 18436
  20.8 45.2 %copy-start.81 = (f32[1536]{0:T(1024)}, f32[1536]{0:T(1024)S(1)}, u32[]{:S(2)}) copy-start(f32[1536]{0:T(1024)S(1)} %get-tuple-element.183) | copy-start | bytes 18436
  376.1 46.8 %copy-start.25 = (f32[2,256,1536]{2,1,0:T(8,128)}, f32[2,256,1536]{2,1,0:T(8,128)S(1)}, u32[]{:S(2)}) copy-start(f32[2,256,1536]{2,1,0:T(8,128)S(1)} %multiply_add_fusion.2) | copy-start | bytes 9437188
  382.2 40.2 %copy-start.30 = (f32[512,1024]{1,0:T(8,128)}, f32[512,1024]{1,0:T(8,128)S(1)}, u32[]{:S(2)}) copy-start(f32[512,1024]{1,0:T(8,128)S(1)} %get-tuple-element.323) | copy-start | bytes 6291460
  436.0 449.0 %reduce-scatter.11.cloned.1.call-start = ((), (), s32[]{:S(2)}) async-start(), calls=%async_computation.8 | async-start | bytes 7077888 | tf_op jit(solution)/shard_map/reduce_scatter | solution.py:242
  481.1 20.9 %copy-start.40 = (f32[2,128,1536]{2,1,0:T(8,128)S(1)}, f32[2,128,1536]{2,1,0:T(8,128)}, u32[]{:S(2)}) copy-start(f32[2,128,1536]{2,1,0:T(8,128)} %slice.652) | copy-start | bytes 4718596
  533.5 36.2 %copy-start.37 = (f32[2,127,1536]{2,1,0:T(8,128)S(1)}, f32[2,127,1536]{2,1,0:T(8,128)}, u32[]{:S(2)}) copy-start(f32[2,127,1536]{2,1,0:T(8,128)} %slice.646) | copy-start | bytes 4681732
  536.6 41.0 %copy-start.38 = (f32[2,127,1536]{2,1,0:T(8,128)S(1)}, f32[2,127,1536]{2,1,0:T(8,128)}, u32[]{:S(2)}) copy-start(f32[2,127,1536]{2,1,0:T(8,128)} %slice.708) | copy-start | bytes 4681732
  612.3 356.2 %reduce-scatter.9.cloned.1.call-start = ((), (), s32[]{:S(2)}) async-start(), calls=%async_computation.7 | async-start | bytes 7077888 | tf_op jit(solution)/shard_map/reduce_scatter | solution.py:241
  676.6 95.0 %copy-start.4 = (f32[2,256,1536]{2,1,0:T(8,128)S(1)}, f32[2,256,1536]{2,1,0:T(8,128)}, u32[]{:S(2)}) copy-start(f32[2,256,1536]{2,1,0:T(8,128)} %copy.60) | copy-start | bytes 9437188
  676.6 95.0 %copy-start.80 = (f32[1536]{0:T(1024)S(1)}, f32[1536]{0:T(1024)}, u32[]{:S(2)}) copy-start(f32[1536]{0:T(1024)} %copy-done.79) | copy-start | bytes 18436
  676.6 95.0 %copy-start.82 = (f32[1536]{0:T(1024)S(1)}, f32[1536]{0:T(1024)}, u32[]{:S(2)}) copy-start(f32[1536]{0:T(1024)} %copy-done.81) | copy-start | bytes 18436
  676.6 95.0 %copy-start.85 = (f32[1536]{0:T(1024)S(1)}, f32[1536]{0:T(1024)}, u32[]{:S(2)}) copy-start(f32[1536]{0:T(1024)} %copy-done.83) | copy-start | bytes 18436
  676.6 95.1 %copy-start.89 = (f32[1536]{0:T(1024)S(1)}, f32[1536]{0:T(1024)}, u32[]{:S(2)}) copy-start(f32[1536]{0:T(1024)} %copy-done.87) | copy-start | bytes 18436
  676.6 95.1 %copy-start.92 = (f32[1536]{0:T(1024)S(1)}, f32[1536]{0:T(1024)}, u32[]{:S(2)}) copy-start(f32[1536]{0:T(1024)} %get-tuple-element.317) | copy-start | bytes 18436
  676.6 95.0 %copy-start.95 = (f32[1536]{0:T(1024)S(1)}, f32[1536]{0:T(1024)}, u32[]{:S(2)}) copy-start(f32[1536]{0:T(1024)} %param.32) | copy-start | bytes 18436
  676.6 95.0 %copy-start.101 = (f32[1536]{0:T(1024)S(1)}, f32[1536]{0:T(1024)}, u32[]{:S(2)}) copy-start(f32[1536]{0:T(1024)} %param.29) | copy-start | bytes 18436
  676.6 95.0 %copy-start.103 = (f32[1536]{0:T(1024)S(1)}, f32[1536]{0:T(1024)}, u32[]{:S(2)}) copy-start(f32[1536]{0:T(1024)} %param.33) | copy-start | bytes 18436
  838.6 6.0 collective-permute-start.1
  852.4 326.1 %reduce-scatter.15.cloned.1.call-start = ((), (), s32[]{:S(2)}) async-start(), calls=%async_computation.10 | async-start | bytes 14155776 | tf_op jit(solution)/shard_map/reduce_scatter | solution.py:244
  861.9 526.4 %reduce-scatter.13.cloned.1.call-start = ((), (), s32[]{:S(2)}) async-start(), calls=%async_computation.9 | async-start | bytes 14155776 | tf_op jit(solution)/shard_map/reduce_scatter | solution.py:243
  870.4 727.9 %reduce-scatter.17.cloned.1.call-start = ((), (), s32[]{:S(2)}) async-start(), calls=%async_computation.11 | async-start | bytes 14155776 | tf_op jit(solution)/shard_map/reduce_scatter | solution.py:245
  880.1 881.3 %all-reduce.83.cloned.1.call-start = ((), (), s32[]{:S(2)}) async-start(), calls=%async_computation.13 | async-start | bytes 17301504 | tf_op jit(solution)/shard_map/psum | solution.py:247
  1598.3 256.8 %all-reduce.81.cloned.1.call-start = ((), (), s32[]{:S(2)}) async-start(), calls=%async_computation.12 | async-start | bytes 3145728 | tf_op jit(solution)/shard_map/psum | solution.py:222
  1604.8 156.6 %copy-start.29 = (bf16[2,256,1024]{2,1,0:T(8,128)(2,1)S(1)}, bf16[2,256,1024]{2,1,0:T(8,128)(2,1)}, u32[]{:S(2)}) copy-start(bf16[2,256,1024]{2,1,0:T(8,128)(2,1)} %param.23) | copy-start | bytes 3145732
  1604.8 156.6 %copy-start.134 = (f32[512]{0:T(512)S(1)}, f32[512]{0:T(512)}, u32[]{:S(2)}) copy-start(f32[512]{0:T(512)} %copy-done.133) | copy-start | bytes 6148
  1761.4 57.1 %copy-start.136 = (f32[1,2,2,128]{3,1,2,0:T(2,128)S(1)}, f32[1,2,2,128]{3,1,2,0:T(2,128)}, u32[]{:S(2)}) copy-start(f32[1,2,2,128]{3,1,2,0:T(2,128)} %copy-done.135) | copy-start | bytes 6148
  1761.5 57.1 %copy-start.12 = (f32[512,1024]{1,0:T(8,128)S(1)}, f32[512,1024]{1,0:T(8,128)}, u32[]{:S(2)}) copy-start(f32[512,1024]{1,0:T(8,128)} %copy-done.10) | copy-start | bytes 6291460
  1822.1 37.4 %copy-start.71 = (f32[192,1024]{1,0:T(8,128)S(1)}, f32[192,1024]{1,0:T(8,128)}, u32[]{:S(2)}) copy-start(f32[192,1024]{1,0:T(8,128)} %get-tuple-element.456) | copy-start | bytes 2359300
  (129 other events, 646.5 us)
Sparse Core Ops, SparseCore 0:
  436.1 118.2 reduce-scatter.6
  612.4 119.0 reduce-scatter.10
  852.5 115.8 reduce-scatter.8
  971.9 206.5 reduce-scatter.14
  1181.9 206.3 reduce-scatter.12
  1391.7 206.4 reduce-scatter.16
  1602.6 158.7 all-reduce.82
  1765.0 90.0 all-reduce.80
